TPU v7x, 256 devices: a whole 4x4x8 slice. The times are simulated.
256 devices in a mesh: row: 16 (over x, y), col: 16 (over z, core).
Axes of the slice: x: 4, y: 4, z: 8, core: 2. Of those that a mesh axis runs over, the one named last changes fastest.
Arguments:
- src_points: float32 [73728, 64], P('row'), may hold values from -1.2 to 1.2
- dst_points: float32 [73728, 64], P(('col', 'row')), may hold values from -1.2 to 1.2
- dst_potential: float32 [73728], P(('col', 'row')), may hold values from -1.2 to 25.3
- partners: int32 [288, 28], P('row'), may hold values from 0 to 287, as said below
- partner_count: int32 [288], P('row'), may hold values from 14 to 28
- src_count: int32 [288], P('row'), may hold values from 64 to 256
- dst_count: int32 [288], P('col'), may hold values from 64 to 256
Outputs:
- src_potential: float32 [73728], P('row')
- dst_new: float32 [73728], P(('col', 'row'))
Inputs may be any that keep to these rules, and one draw needn't show every extreme that they name: `partners`: row s holds 28 different tiles, each within 28 tiles of tile s * 1, counted around the end of the range, except that for even s slot 0 holds tile (s * 1 + 288 // 2) mod 288.
All inputs are finite; a program needn't handle non-finite values.
Results may differ from a plain program's by a relative error of at most 0.00029.
Values sent between devices are 32-bit elements; how exact they have to be, the bound alone decides.
No kernel may reach another device: no remote copies, remote signals or barrier semaphores. Data moves between devices by JAX's collectives and lax.ppermute only.
A program may use at most 128 MiB of HBM per device.

v0:
```python
import math

import jax
import jax.numpy as jnp
from jax import lax
from jax.sharding import PartitionSpec as P

entropy = 0.1
masked_score = -1e30


def joined(part, axis, combine):
    gathered = jax.tree.map(lambda a: lax.all_gather(a, axis), part)

    def take(source):
        return jax.tree.map(lambda a: lax.dynamic_index_in_dim(a, source, 0, False), gathered)

    return lax.fori_loop(
        1, lax.axis_size(axis), lambda source, state: combine(state, take(source)), take(0)
    )


def combine_pairs(first, second):
    highest = jnp.maximum(first[0], second[0])
    summed = first[1] * jnp.exp(first[0] - highest) + second[1] * jnp.exp(second[0] - highest)
    return (highest, summed)


def point_valid(counts, tile):
    places = jnp.arange(tile, dtype=jnp.float32)
    return places[None, :] < counts.astype(jnp.float32)[:, None]


def pick_pairs(flags, src_of, tgt_of, stride, offset, length):
    flags = flags.reshape(-1)
    rank = jnp.cumsum(flags.astype(jnp.int32)) - 1
    mine = flags & (rank % stride == offset)
    place = rank // stride
    wanted = jnp.arange(length, dtype=jnp.int32)
    hit = mine[None, :] & (place[None, :] == wanted[:, None])
    chosen_src = jnp.sum(jnp.where(hit, src_of.reshape(-1)[None, :], 0), axis=1)
    chosen_tgt = jnp.sum(jnp.where(hit, tgt_of.reshape(-1)[None, :], 0), axis=1)
    return (chosen_src, chosen_tgt, jnp.any(hit, axis=1))


def fold_into(carry, high, total, index, valid):
    acc_high, acc_total = carry
    onehot = valid[:, None] & (
        index[:, None] == jnp.arange(acc_high.shape[0], dtype=jnp.int32)[None, :]
    )
    group_high = jnp.max(jnp.where(onehot[:, :, None], high[:, None, :], masked_score), axis=0)
    new_high = jnp.maximum(acc_high, group_high)
    lifted = total[:, None, :] * jnp.exp(jnp.minimum(high[:, None, :] - new_high[None, :, :], 0.0))
    added = jnp.sum(jnp.where(onehot[:, :, None], lifted, 0.0), axis=0)
    return (new_high, acc_total * jnp.exp(acc_high - new_high) + added)


def sweep(picks, begin, visit):

    def turn(carry, item):
        src_pick, tgt_pick, valid = item
        return (
            lax.cond(
                jnp.any(valid),
                lambda held: visit(held, src_pick, tgt_pick, valid),
                lambda held: held,
                carry,
            ),
            None,
        )

    result, unused = lax.scan(turn, begin, picks)
    return result


def shards(src_points, dst_points, dst_potential, partners, partner_count, src_count, dst_count):
    src_tile_count = src_count.shape[0]
    dst_tile_count = dst_count.shape[0]
    tile = src_points.shape[0] // src_tile_count
    depth = src_points.shape[1]
    slot_count = partners.shape[1]
    row_devices = lax.axis_size("row")
    col_devices = lax.axis_size("col")
    num_src_tiles = src_tile_count * row_devices
    num_dst_tiles = dst_tile_count * col_devices
    targets, potential = (
        lax.all_gather(dst_points, "row", axis=0, tiled=True),
        lax.all_gather(dst_potential, "row", axis=0, tiled=True),
    )
    count_values = dst_count.astype(jnp.float32)
    slot_on = jnp.arange(slot_count, dtype=jnp.int32)[None, :] < partner_count[:, None]
    src_index = jnp.broadcast_to(
        jnp.arange(src_tile_count, dtype=jnp.int32)[:, None], partners.shape
    )
    col_here = lax.axis_index("col")
    row_here = lax.axis_index("row")
    held_points = targets.reshape(-1, tile, depth)
    held_values = potential.reshape(-1, tile)
    flags = slot_on & (partners // dst_tile_count == col_here)
    local_target = partners - col_here * dst_tile_count
    stride = 1
    offset = 0
    capacity = src_tile_count * min(slot_count, dst_tile_count)
    group = max(min(capacity, 12), -(-capacity // 24))
    turns = -(-capacity // group)
    chosen_src, chosen_tgt, chosen_valid = pick_pairs(
        flags, src_index, local_target, stride, offset, group * turns
    )
    picks = (
        chosen_src.reshape(turns, group),
        chosen_tgt.reshape(turns, group),
        chosen_valid.reshape(turns, group),
    )
    src_tiles = src_points.reshape(src_tile_count, tile, depth)
    src_half = 0.5 * jnp.sum(src_tiles * src_tiles, axis=2)
    held_half = 0.5 * jnp.sum(held_points * held_points, axis=2)
    held_live = point_valid(count_values, tile)
    src_live = point_valid(src_count, tile)

    def pair_cost(src_pick, tgt_pick):
        rows = src_tiles[src_pick]
        columns = held_points[tgt_pick]
        cross = jnp.einsum(
            "gid,gjd->gij",
            rows,
            columns,
            precision=lax.Precision.HIGHEST,
            preferred_element_type=jnp.float32,
        )
        return src_half[src_pick][:, :, None] + held_half[tgt_pick][:, None, :] - cross

    def row_visit(carry, src_pick, tgt_pick, valid):
        cost = pair_cost(src_pick, tgt_pick)
        live = valid[:, None, None] & held_live[tgt_pick][:, None, :]
        score = jnp.where(live, (held_values[tgt_pick][:, None, :] - cost) / entropy, masked_score)
        high = jnp.max(score, axis=2)
        total = jnp.sum(jnp.where(live, jnp.exp(score - high[:, :, None]), 0.0), axis=2)
        return fold_into(carry, high, total, src_pick, valid)

    start_rows = (
        jnp.full((src_tile_count, tile), masked_score, jnp.float32),
        jnp.zeros((src_tile_count, tile), jnp.float32),
    )
    row_high, row_total = sweep(picks, start_rows, row_visit)
    row_high = row_high.reshape(-1)
    row_total = row_total.reshape(-1)
    overall = lax.pmax(row_high, "col")
    row_total = lax.psum(row_total * jnp.exp(row_high - overall), "col")
    row_high = overall
    src_mass = jnp.repeat(-jnp.log(src_count.astype(jnp.float32)), tile) - math.log(num_src_tiles)
    src_potential = jnp.where(
        src_live.reshape(-1), entropy * (src_mass - (row_high + jnp.log(row_total))), 0.0
    )
    src_values = src_potential.reshape(src_tile_count, tile)

    def column_visit(carry, src_pick, tgt_pick, valid):
        cost = pair_cost(src_pick, tgt_pick)
        live = valid[:, None, None] & src_live[src_pick][:, :, None]
        score = jnp.where(live, (src_values[src_pick][:, :, None] - cost) / entropy, masked_score)
        high = jnp.max(score, axis=1)
        total = jnp.sum(jnp.where(live, jnp.exp(score - high[:, None, :]), 0.0), axis=1)
        return fold_into(carry, high, total, tgt_pick, valid)

    held_tiles = held_points.shape[0]
    start_columns = (
        jnp.full((held_tiles, tile), masked_score, jnp.float32),
        jnp.zeros((held_tiles, tile), jnp.float32),
    )
    col_high, col_total = sweep(picks, start_columns, column_visit)
    col_high = col_high.reshape(-1)
    col_total = col_total.reshape(-1)
    share = dst_tile_count * tile // row_devices
    start = row_here * share
    merged_high, merged_total = joined((col_high, col_total), "row", combine_pairs)
    mine_high = lax.dynamic_slice_in_dim(merged_high, start, share, 0)
    mine_total = lax.dynamic_slice_in_dim(merged_total, start, share, 0)
    dst_mass = jnp.repeat(-jnp.log(count_values), tile) - math.log(num_dst_tiles)
    mine_mass = lax.dynamic_slice_in_dim(dst_mass, start, share, 0)
    mine_valid = lax.dynamic_slice_in_dim(point_valid(dst_count, tile).reshape(-1), start, share, 0)
    col_lse = mine_high + jnp.log(jnp.maximum(mine_total, 1.0))
    dst_new = jnp.where(mine_valid & (mine_total > 0.0), entropy * (mine_mass - col_lse), 0.0)
    return (src_potential, dst_new)


def solution(mesh):
    in_specs = (
        P("row", None),
        P(("col", "row"), None),
        P(("col", "row")),
        P("row", None),
        P("row"),
        P("row"),
        P("col"),
    )
    out_specs = (P("row"), P(("col", "row")))
    return jax.shard_map(shards, mesh=mesh, in_specs=in_specs, out_specs=out_specs, check_vma=False)
```

profile of v0, /device:TPU:6, one launch (start us, length us, event | category | flops | bytes accessed | tf_op | source)
XLA Modules:
  0.0 654.2 jit_solution(83088639271929644)
XLA Ops:
  7.2 0.7 all-gather.5.cloned.1.call-update
  7.9 0.8 fusion.17
  8.8 0.7 broadcast_subtract_fusion
  11.2 1.3 dynamic-slice
  13.2 0.9 dynamic-update-slice
  14.1 67.3 %all-reduce.1 = f32[4608]{0:T(1024)S(1)} all-reduce(f32[4608]{0:T(1024)S(1)} %dynamic-update-slice), channel_id=1, replica_groups=mesh['row'=16,'col'=16] {'row'}, use_global_device_ids=true, to_apply=%add.1 | all-reduce | flops 4608 | bytes 36864
  81.4 2.9 copy.42
  84.8 1.6 multiply_reduce_fusion
  86.5 3.0 copy.50
  89.5 32.2 %while.44 = (s32[]{:T(128)}, f32[18,256]{1,0:T(8,128)S(1)}, f32[18,256]{1,0:T(8,128)S(1)}, pred[24,14]{1,0:T(8,128)(4,1)S(1)}, s32[24,14]{1,0:T(8,128)S(1)}, /*i...) while((s32[]{:T(128)}, f32[18,256]{1,0:T(8,128)S(1)}, ...), condition=%wide.region_15.16_spmd.clone, body=%wide.region_7.15_spmd.clone.sunk | while | flops 717952576 | bytes 13415899 | solution.py:72
  89.5 0.6 fusion.27
  90.8 0.6 fusion.27
  92.2 0.6 fusion.27
  93.5 0.6 fusion.27
  94.9 0.6 fusion.27
  96.2 0.6 fusion.27
  97.5 0.6 fusion.27
  98.9 0.6 fusion.27
  100.2 0.6 fusion.27
  101.6 0.6 fusion.27
  102.9 0.6 fusion.27
  104.3 0.6 fusion.27
  105.6 0.6 fusion.27
  106.9 0.6 fusion.27
  108.3 0.6 fusion.27
  109.6 0.6 fusion.27
  111.0 0.6 fusion.27
  112.3 0.6 fusion.27
  113.6 0.6 fusion.27
  115.0 0.6 fusion.27
  116.3 0.6 fusion.27
  117.7 0.6 fusion.27
  119.0 0.6 fusion.27
  120.3 0.6 fusion.27
  121.7 220.7 %pmax.7 = f32[4608]{0:T(1024)S(1)} all-reduce(f32[4608]{0:T(1024)S(1)} %reshape.314), channel_id=1, replica_groups=mesh['row'=16,'col'=16] {'col'}, use_global_device_ids=true, to_apply=%region_16.17 | all-reduce | flops 4608 | bytes 36864 | tf_op jit(solution)/shard_map/pmax | solution.py:147
  342.4 45.7 %psum.7 = f32[4608]{0:T(1024)S(1)} all-reduce(f32[4608]{0:T(1024)S(1)} %exponential_multiply_fusion), channel_id=1, replica_groups=mesh['row'=16,'col'=16] {'col'}, use_global_device_ids=true, to_apply=%region_17.18 | all-reduce | flops 4608 | bytes 36864 | tf_op jit(solution)/shard_map/psum | solution.py:148
  388.7 32.2 %while.45 = (s32[]{:T(128)}, f32[18,256]{1,0:T(8,128)S(1)}, f32[18,256]{1,0:T(8,128)S(1)}, pred[24,14]{1,0:T(8,128)(4,1)S(1)}, s32[24,14]{1,0:T(8,128)S(1)}, /*i...) while((s32[]{:T(128)}, f32[18,256]{1,0:T(8,128)S(1)}, ...), condition=%wide.region_26.27_spmd.clone, body=%wide.region_18.26_spmd.clone.sunk | while | flops 717952576 | bytes 13415899 | solution.py:72
  390.1 0.6 fusion.28
  391.4 0.6 fusion.28
  392.8 0.6 fusion.28
  394.1 0.6 fusion.28
  395.4 0.6 fusion.28
  396.8 0.6 fusion.28
  398.1 0.6 fusion.28
  399.5 0.6 fusion.28
  400.8 0.6 fusion.28
  402.2 0.6 fusion.28
  403.5 0.6 fusion.28
  404.8 0.6 fusion.28
  406.2 0.6 fusion.28
  407.5 0.6 fusion.28
  408.9 0.6 fusion.28
  410.2 0.6 fusion.28
  411.5 0.6 fusion.28
  412.9 0.6 fusion.28
  414.2 0.6 fusion.28
  415.6 0.6 fusion.28
  416.9 0.6 fusion.28
  418.3 0.6 fusion.28
  419.6 0.6 fusion.28
  421.0 202.3 %all-gather.2 = f32[16,1,4608]{2,1,0:T(1,128)S(1)} all-gather(f32[1,1,4608]{2,1,0:T(1,128)S(1)} %reshape.421), channel_id=1, replica_groups=mesh['row'=16,'col'=16] {'row'}, dimensions={0}, use_global_device_ids=true | all-gather | bytes 313344 | tf_op jit(solution)/shard_map/all_gather | solution.py:13
  623.4 20.8 %all-gather.1 = f32[16,1,4608]{2,1,0:T(1,128)S(1)} all-gather(f32[1,1,4608]{2,1,0:T(1,128)S(1)} %reshape.419), channel_id=1, replica_groups=mesh['row'=16,'col'=16] {'row'}, dimensions={0}, use_global_device_ids=true | all-gather | bytes 313344 | tf_op jit(solution)/shard_map/all_gather | solution.py:13
  644.3 2.4 while.43
  646.7 0.7 multiply_select_fusion.3
  (187 shorter events, 7.0 us)
Async XLA Ops:
  7.2 77.1 %copy-start = (f32[4608,64]{0,1:T(8,128)S(1)}, f32[4608,64]{0,1:T(8,128)}, u32[]{:S(2)}) copy-start(f32[4608,64]{0,1:T(8,128)} %param.17) | copy-start | bytes 3538948
  7.2 77.3 %copy-start.3 = (s32[18]{0:T(128)S(1)}, s32[18]{0:T(128)}, u32[]{:S(2)}) copy-start(s32[18]{0:T(128)} %param.23) | copy-start | bytes 220
  7.2 77.3 %copy-start.2 = (s32[18]{0:T(128)S(1)}, s32[18]{0:T(128)}, u32[]{:S(2)}) copy-start(s32[18]{0:T(128)} %param.22) | copy-start | bytes 220
  7.2 77.6 %all-gather.5.cloned.1.call-start = ((), (), s32[]{:S(2)}) async-start(), calls=%async_computation | async-start | bytes 1671168 | tf_op jit(solution)/shard_map/all_gather | solution.py:87
  388.1 0.6 copy-start.1
Sparse Core Ops, SparseCore 0:
  10.5 51.5 all-gather.4
where the time goes:
time: 660 us; the launch traced here: 654 us
  blocking collectives  557 us (84%)
  other arithmetic  36.3 us (5%)
  loops' own time  33.6 us (5%)
  between operations  15 us (2%)
  local copies, waits for them, and re-layouts  11.8 us (2%)
    all_gather x2, blocking collectives, joined(): gathered = jax.tree.map(lambda a: lax.all_gather(a, axis), part)  223 us
    pmax x1, blocking collectives, shards(): overall = lax.pmax(row_high, 'col')  221 us
    unnamed x1, blocking collectives  67.3 us
    psum x1, blocking collectives, shards(): row_total = lax.psum(row_total * jnp.exp(row_high - overall), 'col')  45.7 us
    another operation x2, loops' own time, sweep(): result, unused = lax.scan(turn, begin, picks)  32.4 us
    reduce_or x48, other arithmetic, turn(): jnp.any(valid)  30.8 us
  transfers between devices with their start and end apart: 1, of which 0 were waited for; matrix products, arithmetic and copies ran while one was open for 1% of the time, Pallas kernels for 0%

commit v1 on v0

v1 whole, which is shorter than its diff:
```python
import functools
import math

import jax
import jax.numpy as jnp
from jax import lax
from jax.experimental import pallas as pl
from jax.experimental.pallas import tpu as pltpu
from jax.sharding import PartitionSpec as P

entropy = 0.1
scale = math.log2(math.e) / entropy
ln2 = math.log(2.0)
nothing = -1e30
floor = -1e25
half = 128
wire_rows = 152
f32 = jnp.float32
bf16 = jnp.bfloat16


def pieces(a):
    first = a.astype(bf16).astype(f32)
    rest = a - first
    second = rest.astype(bf16).astype(f32)
    return first, second, rest - second


def extra_rows(bias):
    place = lax.broadcasted_iota(jnp.int32, (64, bias.shape[1]), 0)
    first, second, third = pieces(bias)
    block = jnp.where(place < 3, 1.0, 0.0)
    for k, piece in enumerate((first, second, third)):
        block = jnp.where(place == 3 + k, piece, block)
    return block.astype(bf16)


def prepare_sources(points_ref, main_ref, bias_ref):
    tiles, depth, tile = main_ref.shape
    for s in range(tiles):
        x = points_ref[:, s * tile : (s + 1) * tile]
        high = x.astype(bf16)
        low = (x - high.astype(f32)).astype(bf16)
        bias = (-0.5 * scale) * jnp.sum(x * x, axis=0, keepdims=True)
        main_ref[s, 0:64, :] = high
        main_ref[s, 64:128, :] = high
        main_ref[s, 128:192, :] = low
        main_ref[s, 192:256, :] = extra_rows(bias)
        bias_ref[s : s + 1, :] = bias


def unpack_targets(wire_ref, operand_ref):
    shards_held = wire_ref.shape[0]
    lane = lax.broadcasted_iota(jnp.int32, (144, 128), 1)
    front = lane < 64
    sublane = lax.broadcasted_iota(jnp.int32, (16, 256), 0)
    pick = (
        lax.broadcasted_iota(jnp.int32, (16, 128), 1)
        == lax.broadcasted_iota(jnp.int32, (16, 128), 0) + 64
    ) & (lax.broadcasted_iota(jnp.int32, (16, 128), 0) < 6)
    pick = jnp.where(pick, 1.0, 0.0).astype(bf16)

    def columns(row):
        first, second, third = pieces(row)
        stacked = jnp.where(sublane < 6, 1.0, 0.0)
        for k, piece in enumerate((first, second, third)):
            stacked = jnp.where(sublane == k, piece, stacked)
        return lax.dot_general(
            stacked.astype(bf16), pick, (((0,), (0,)), ((), ())), preferred_element_type=f32
        )[0:144]

    def one(m, carry):
        both = wire_ref[m, 0:144, :]
        high = both.astype(bf16).astype(f32)
        low = both - high
        high_back = pltpu.roll(high, 64, 1)
        low_back = pltpu.roll(low, 64, 1)
        tail = wire_ref[m, 144:152, :]
        extra_a = columns(jnp.concatenate([tail[0:1], tail[1:2]], axis=1))
        extra_b = columns(jnp.concatenate([tail[2:3], tail[3:4]], axis=1))
        start = pl.multiple_of(m * 288, 16)
        after = pl.multiple_of(m * 288 + 144, 16)
        operand_ref[pl.ds(start, 144), 0:128] = jnp.where(front, high, low_back).astype(bf16)
        operand_ref[pl.ds(start, 144), 128:256] = jnp.where(front, high, extra_a).astype(bf16)
        operand_ref[pl.ds(after, 144), 0:128] = jnp.where(front, high_back, low).astype(bf16)
        operand_ref[pl.ds(after, 144), 128:256] = jnp.where(front, high_back, extra_b).astype(bf16)
        return carry

    lax.fori_loop(0, shards_held, one, 0)
    rows = shards_held * 288
    dummy_lane = lax.broadcasted_iota(jnp.int32, (half, 256), 1)
    operand_ref[rows : rows + half, :] = jnp.where(dummy_lane == 192, nothing, 0.0).astype(bf16)


def row_pass(count_ref, list_ref, wire_ref, main_ref, lse_ref, operand_ref):
    tiles, depth, tile = main_ref.shape
    unpack_targets(wire_ref, operand_ref)

    def one_tile(s, carry):
        weights = main_ref[s]

        def score(unit):
            rows = operand_ref[pl.ds(pl.multiple_of(unit * half, half), half), :]
            return jnp.dot(rows, weights, preferred_element_type=f32).reshape(half // 8, 8, tile)

        def step(i, state):
            high, total = state
            one = score(list_ref[s, 2 * i])
            two = score(list_ref[s, 2 * i + 1])
            new = jnp.maximum(high, jnp.maximum(jnp.max(one, axis=0), jnp.max(two, axis=0)))
            total = total * jnp.exp2(high - new)
            total = total + jnp.sum(jnp.exp2(one - new[None]), axis=0)
            total = total + jnp.sum(jnp.exp2(two - new[None]), axis=0)
            return new, total

        start = (jnp.full((8, tile), floor, f32), jnp.zeros((8, tile), f32))
        high, total = lax.fori_loop(0, (count_ref[s] + 1) // 2, step, start)
        top = jnp.max(high, axis=0, keepdims=True)
        total = jnp.sum(total * jnp.exp2(high - top), axis=0, keepdims=True)
        lse_ref[pl.ds(s, 1), :] = jnp.where(
            total > 0.0, top + jnp.log2(jnp.maximum(total, 1e-30)), nothing
        )
        return carry

    lax.fori_loop(0, tiles, one_tile, 0)


def column_pass(
    count_ref, list_ref, live_ref, main_ref, operand_ref, bias_ref, out_ref,
    weights_ref, total_ref, high_ref, seen_ref,
):
    tiles, depth, tile = main_ref.shape
    units = out_ref.shape[0]

    def clear(u, carry):
        total_ref[pl.ds(pl.multiple_of(u * half, half), half), :] = jnp.zeros((half, 128), f32)
        seen_ref[u] = 0
        return carry

    def sweep(visit):
        def one_tile(s, carry):
            weights_ref[0:192, :] = main_ref[s, 0:192, :]
            weights_ref[192:256, :] = extra_rows(bias_ref[pl.ds(s, 1), :])

            def step(i, inner):
                for k in range(2):
                    unit = list_ref[s, 2 * i + k]
                    where = pl.ds(pl.multiple_of(unit * half, half), half)
                    visit(
                        unit,
                        where,
                        jnp.dot(
                            operand_ref[where, :], weights_ref[...], preferred_element_type=f32
                        ),
                    )
                return inner

            lax.fori_loop(0, (count_ref[s] + 1) // 2, step, 0)
            return carry

        lax.fori_loop(0, tiles, one_tile, 0)

    def add(unit, where, score):
        part = jnp.exp2(score)
        total_ref[where, :] += part[:, 0:128] + part[:, 128:256]
        seen_ref[unit] = 1

    lax.fori_loop(0, units + 1, clear, 0)
    sweep(add)
    ones = jnp.ones((8, 128), f32)
    lane = lax.broadcasted_iota(jnp.int32, (8, 128), 1)

    def lane_sums(block):
        return lax.dot_general(
            ones,
            block,
            (((1,), (1,)), ((), ())),
            precision=lax.Precision.HIGHEST,
            preferred_element_type=f32,
        )

    def finish(u, bad):
        where = pl.ds(pl.multiple_of(u * half, half), half)
        sums = lane_sums(total_ref[where, :])
        out_ref[pl.ds(u, 1), :] = jnp.where(
            sums > 0.0, jnp.log2(jnp.maximum(sums, 1e-37)), nothing
        )[0:1]
        needed = jnp.where(seen_ref[u] > 0, live_ref[u], 0)
        return jnp.maximum(bad, jnp.where((lane < needed) & (sums < 1e-25), 1.0, 0.0))

    bad = lax.fori_loop(0, units, finish, jnp.zeros((8, 128), f32))

    @pl.when(jnp.max(bad) > 0.0)
    def _():
        def clear_both(u, carry):
            where = pl.ds(pl.multiple_of(u * half, half), half)
            total_ref[where, :] = jnp.zeros((half, 128), f32)
            high_ref[where, :] = jnp.full((half, 128), floor, f32)
            return carry

        def add_safely(unit, where, score):
            one, two = score[:, 0:128], score[:, 128:256]
            old = high_ref[where, :]
            new = jnp.maximum(old, jnp.maximum(one, two))
            high_ref[where, :] = new
            total_ref[where, :] = (
                total_ref[where, :] * jnp.exp2(old - new)
                + jnp.exp2(one - new)
                + jnp.exp2(two - new)
            )

        def finish_safely(u, carry):
            where = pl.ds(pl.multiple_of(u * half, half), half)
            high = high_ref[where, :]
            top = jnp.max(high, axis=1, keepdims=True)
            sums = lane_sums(total_ref[where, :] * jnp.exp2(high - top))
            tops = lane_sums(jnp.where(lax.broadcasted_iota(jnp.int32, (half, 128), 1) == 0, top, 0.0))
            out_ref[pl.ds(u, 1), :] = jnp.where(
                sums > 0.0, tops + jnp.log2(jnp.maximum(sums, 1e-37)), nothing
            )[0:1]
            return carry

        lax.fori_loop(0, units + 1, clear_both, 0)
        sweep(add_safely)
        lax.fori_loop(0, units, finish_safely, 0)


def log_sum(parts):
    top = functools.reduce(jnp.maximum, parts)
    total = sum(jnp.exp2(p - top) for p in parts)
    return top + jnp.log2(total)


def shards(src_points, dst_points, dst_potential, partners, partner_count, src_count, dst_count):
    src_tiles = src_count.shape[0]
    dst_tiles = dst_count.shape[0]
    tile = src_points.shape[0] // src_tiles
    slots = partners.shape[1]
    rows = lax.axis_size("row")
    cols = lax.axis_size("col")
    row_here = lax.axis_index("row")
    col_here = lax.axis_index("col")
    share = dst_points.shape[0]
    units = 2 * dst_tiles
    smem = pl.BlockSpec(memory_space=pltpu.SMEM)
    vmem = pl.BlockSpec(memory_space=pltpu.VMEM)
    params = pltpu.CompilerParams(vmem_limit_bytes=48 * 1024 * 1024)

    spot = row_here * share + jnp.arange(share, dtype=jnp.int32)
    spot_tile = spot // tile
    spot_count = jnp.sum(
        jnp.where(
            spot_tile[:, None] == jnp.arange(dst_tiles, dtype=jnp.int32)[None, :],
            dst_count[None, :],
            0,
        ),
        axis=1,
    )
    mine_valid = spot - spot_tile * tile < spot_count
    level = scale * (dst_potential - 0.5 * jnp.sum(dst_points * dst_points, axis=1))
    level = jnp.where(mine_valid, level, nothing)
    mid = share // 2
    packed = scale * jnp.concatenate([dst_points[:mid], dst_points[mid:]], axis=1)
    tail = jnp.pad(level.reshape(2, mid), ((0, 0), (0, 256 - mid))).reshape(4, 128)
    wire = jnp.concatenate([packed, tail, jnp.zeros((4, 128), f32)], axis=0)
    gathered = lax.all_to_all(
        jnp.broadcast_to(wire[None], (rows,) + wire.shape), "row", 0, 0
    )

    main, bias = pl.pallas_call(
        prepare_sources,
        out_shape=(
            jax.ShapeDtypeStruct((src_tiles, 256, tile), bf16),
            jax.ShapeDtypeStruct((src_tiles, tile), f32),
        ),
        in_specs=[vmem],
        out_specs=(vmem, vmem),
        compiler_params=params,
    )(src_points.T)

    slot_on = jnp.arange(slots, dtype=jnp.int32)[None, :] < partner_count[:, None]
    local = jnp.where(slot_on, partners - col_here * dst_tiles, -1)
    unit_ids = jnp.arange(units, dtype=jnp.int32)
    live = jnp.clip(
        jnp.repeat(dst_count, 2) - (unit_ids % 2) * half, 0, half
    )
    active = jnp.any(local[:, :, None] == (unit_ids // 2)[None, None, :], axis=1) & (live > 0)[None, :]
    earlier = (unit_ids[:, None] < unit_ids[None, :]).astype(jnp.int32)
    rank = jnp.sum(jnp.where(active[:, :, None], earlier[None], 0), axis=1)
    counts = jnp.sum(active.astype(jnp.int32), axis=1)
    order = jnp.arange(units + 4, dtype=jnp.int32)
    listed = jnp.sum(
        jnp.where(
            active[:, :, None] & (rank[:, :, None] == order[None, None, :]),
            unit_ids[None, :, None],
            0,
        ),
        axis=1,
    )
    listed = jnp.where(order[None, :] < counts[:, None], listed, units)

    lse, operand = pl.pallas_call(
        row_pass,
        out_shape=(
            jax.ShapeDtypeStruct((src_tiles, tile), f32),
            jax.ShapeDtypeStruct((dst_tiles * tile + half, 256), bf16),
        ),
        in_specs=[smem, smem, vmem, vmem],
        out_specs=(vmem, vmem),
        compiler_params=params,
    )(counts, listed, gathered, main)

    reach = -(-slots // dst_tiles)
    steps = [d % cols for d in range(-reach, reach + 1)] + [cols // 2]
    idle = [d for d in range(cols) if d not in steps]
    mates = len(steps)

    def to(row, src, dst):
        return (row * cols + (row + src) % cols, row * cols + (row + dst) % cols)

    parts = [lse]
    for turn in range(1, mates):
        hops = [
            to(r, steps[a], steps[(a + turn) % mates]) for r in range(rows) for a in range(mates)
        ]
        parts.append(lax.ppermute(lse, ("row", "col"), hops))
    row_lse = log_sum(parts)
    counted = src_count.astype(f32)
    place = jnp.arange(tile, dtype=jnp.int32)
    src_live = place[None, :] < src_count[:, None]
    all_src = src_tiles * rows
    potential = jnp.where(
        src_live,
        entropy * (-jnp.log(counted)[:, None] - math.log(all_src) - ln2 * row_lse),
        0.0,
    )
    shared = potential.reshape(-1)
    member = functools.reduce(
        jnp.logical_or, [(col_here - row_here) % cols == d for d in steps]
    )
    src_potential = jnp.where(member, shared, 0.0)
    for begin in range(0, len(idle), mates):
        chunk = idle[begin : begin + mates]
        hops = [to(r, steps[a], d) for r in range(rows) for a, d in enumerate(chunk)]
        got = lax.ppermute(shared, ("row", "col"), hops)
        here = functools.reduce(
            jnp.logical_or, [(col_here - row_here) % cols == d for d in chunk]
        )
        src_potential = jnp.where(here, got, src_potential)

    mass_bias = jnp.where(
        src_live,
        bias - row_lse - jnp.log2(counted)[:, None] - math.log2(all_src),
        nothing,
    )
    col_part = pl.pallas_call(
        column_pass,
        out_shape=jax.ShapeDtypeStruct((units, half), f32),
        in_specs=[smem, smem, smem, vmem, vmem, vmem],
        out_specs=vmem,
        scratch_shapes=[
            pltpu.VMEM((256, tile), bf16),
            pltpu.VMEM((dst_tiles * tile + half, 128), f32),
            pltpu.VMEM((dst_tiles * tile + half, 128), f32),
            pltpu.SMEM((units + 1,), jnp.int32),
        ],
        compiler_params=params,
    )(counts, listed, live, main, operand, mass_bias)

    shared_out = lax.all_to_all(col_part.reshape(rows, share), "row", 0, 0)
    top = jnp.max(shared_out, axis=0)
    col_log = top + jnp.log2(jnp.sum(jnp.exp2(shared_out - top[None]), axis=0))
    dst_new = jnp.where(
        mine_valid & (top > 0.5 * nothing),
        entropy
        * (-jnp.log(spot_count.astype(f32)) - math.log(dst_tiles * cols) - ln2 * col_log)
        + dst_potential,
        0.0,
    )
    return src_potential, dst_new


def solution(mesh):
    in_specs = (
        P("row", None),
        P(("col", "row"), None),
        P(("col", "row")),
        P("row", None),
        P("row"),
        P("row"),
        P("col"),
    )
    out_specs = (P("row"), P(("col", "row")))
    return jax.shard_map(shards, mesh=mesh, in_specs=in_specs, out_specs=out_specs, check_vma=False)
```

time: 660 us -> 181 us (0.27)
  blocking collectives: 557 us -> 0 us
  starting transfers between devices: 0.04 us -> 112 us
  waiting for transfers between devices: 0.68 us -> 38.1 us
  loops' own time: 33.6 us -> 0 us
  other arithmetic: 36.3 us -> 6.75 us
  Pallas kernels: 0 us -> 16 us
  between operations: 15 us -> 0.95 us
    all_gather x2 -> x0, blocking collectives: 223 us -> none  [joined(): gathered = jax.tree.map(lambda a: lax.all_gather(a, axis), part)]
    pmax x1 -> x0, blocking collectives: 221 us -> none  [shards(): overall = lax.pmax(row_high, 'col')]
    all_to_all x0 -> x2, starting transfers between devices: none -> 106 us  [the longest x1 98.8 us: shards(): shared_out = lax.all_to_all(col_part.reshape(rows, share), 'row', 0, 0)]
    unnamed x1 -> x0, blocking collectives: 67.3 us -> none
    psum x1 -> x0, blocking collectives: 45.7 us -> none  [shards(): row_total = lax.psum(row_total * jnp.exp(row_high - overall), 'col')]
    another operation x51 -> x0, loops' own time: 33.6 us -> none  [the longest x2 32.4 us: sweep(): result, unused = lax.scan(turn, begin, picks)]
    reduce_or x49 -> x1, other arithmetic: 31 us -> 0.82 us  [shards(): jnp.any(local[:, :, None] == (unit_ids // 2)[None, None, :], axis=1)]
    ppermute x0 -> x7, waiting for transfers between devices: none -> 20.8 us  [the longest x2 20.8 us: shards(): got = lax.ppermute(shared, ('row', 'col'), hops)]
  transfers between devices with their start and end apart: 1 -> 9, of which waited for: 0 -> 3; matrix products, arithmetic and copies ran while one was open for 1% -> 2% of each run, Pallas kernels for 0% -> 0%
where the time goes in v1:
time: 181 us; the launch traced here: 180 us
  starting transfers between devices  112 us (62%)
  waiting for transfers between devices  38.1 us (21%)
  Pallas kernels  16 us (9%)
  local copies, waits for them, and re-layouts  7.06 us (4%)
  other arithmetic  6.75 us (4%)
    all_to_all x1, starting transfers between devices, shards(): shared_out = lax.all_to_all(col_part.reshape(rows, share), 'row', 0, 0)  98.8 us
    ppermute x2, waiting for transfers between devices, shards(): got = lax.ppermute(shared, ('row', 'col'), hops)  20.8 us
    all_to_all x1, waiting for transfers between devices, shards(): lax.all_to_all(jnp.broadcast_to(wire[None], (rows,) + wire.shape), 'row',...  13.8 us
    pallas_call x1, Pallas kernels, shards(): pl.pallas_call(column_pass, out_shape=jax.ShapeDtypeStruct((units, half),...  9.69 us
    all_to_all x1, starting transfers between devices, shards(): lax.all_to_all(jnp.broadcast_to(wire[None], (rows,) + wire.shape), 'row',...  7.57 us
    pallas_call x1, Pallas kernels, shards(): pl.pallas_call(row_pass, out_shape=(jax.ShapeDtypeStruct((src_tiles, tile...  5.93 us
  transfers between devices with their start and end apart: 9, of which 3 were waited for; matrix products, arithmetic and copies ran while one was open for 2% of the time, Pallas kernels for 0%

profile of v1, /device:TPU:6, one launch (start us, length us, event | category | flops | bytes accessed | tf_op | source)
XLA Modules:
  0.0 180.5 jit_solution(5604573698578102548)
XLA Ops:
  0.6 0.9 multiply_reduce_fusion
  1.6 1.0 fusion.14
  2.6 0.7 select_reduce_fusion.2
  3.3 0.7 multiply_select_fusion.1
  4.0 0.1 reshape.110
  4.1 0.1 copy.15
  4.3 0.1 pad.7.clone
  4.3 0.1 maximum_maximum_fusion
  4.4 0.1 copy.16
  4.5 1.1 broadcast_in_dim.117
  5.7 0.0 copy-start.5
  5.7 0.0 copy-start.8
  5.7 0.0 copy-start.2
  5.7 7.6 %all-to-all-start = ((f32[16,152,128]{2,1,0:T(8,128)}), f32[16,152,128]{2,1,0:T(8,128)}, u32[]{:S(2)}, u32[]{:S(2)}) async-start(f32[16,152,128]{2,1,0:T(8,128)} %broadcast_in_dim.117), calls=%async_computation | async-start | bytes 2490368 | tf_op jit(solution)/shard_map/all_to_all | solution.py:266
  13.3 0.0 copy-done.5
  13.3 0.0 copy-done.9
  13.3 0.1 subtract_select_fusion
  13.3 0.5 and_select_fusion.1
  13.9 0.0 copy-done.8
  13.9 0.1 broadcast_in_dim.106
  13.9 0.6 reshape.109
  14.5 0.0 copy-done.2
  14.5 0.3 shard_map.86
  14.9 0.0 copy-start.3
  14.9 0.8 compare_reduce_fusion
  15.7 0.7 broadcast_compare_fusion
  16.4 0.1 convert_reduce_fusion
  16.5 0.2 select_reduce_fusion.1
  16.7 0.4 select_reduce_fusion
  17.1 0.0 copy-done.3
  17.1 0.1 fusion.5.list_ref
  17.2 13.8 %all-to-all-done.wire_ref = f32[16,152,128]{2,1,0:T(8,128)} async-done(((f32[16,152,128]{2,1,0:T(8,128)}), f32[16,152,128]{2,1,0:T(8,128)}, u32[]{:S(2)}, u32[]{:S(2)}) %all-to-all-start) | async-done | bytes 1245216 | tf_op jit(solution)/shard_map/all_to_all | solution.py:266
  31.0 0.0 copy-start.7
  31.0 0.0 copy-start.4
  31.0 5.9 %shard_map.87 = (f32[18,256]{1,0:T(8,128)S(1)}, bf16[4736,256]{1,0:T(8,128)(2,1)S(1)}) custom-call(s32[18]{0:T(128)S(1)} %get-tuple-element.12.count_ref, s32[18,40]{1,0:T(8,128)S(1)} %fusion.5.list_ref, f32[16,152,128]{2,1,0:T(8,128)} %all-to-all-done.wire_ref, bf16[18,256,256]{2,1,0:T(8,128)(2,1)S(1)} %get-tuple-element.6.main_ref), custom_call_target="tpu_custom_call" | custom-call | tf_op jit(solution)/shard_map/pallas_call | solution.py:302
  36.9 0.0 copy-start
  36.9 1.4 copy-done
  38.3 0.7 collective-permute-start
  39.0 0.7 collective-permute-start.1
  39.7 0.7 collective-permute-start.2
  40.3 0.7 collective-permute-start.3
  41.0 0.7 collective-permute-start.4
  41.7 0.0 copy-done.7
  41.8 0.0 collective-permute-done
  41.8 0.0 collective-permute-done.1
  41.8 0.0 collective-permute-done.2
  41.8 0.0 collective-permute-done.3
  41.8 0.0 collective-permute-done.4
  41.8 0.0 copy-done.4
  41.8 0.1 add_select_fusion
  41.9 0.0 copy-start.1
  41.9 1.7 copy-done.1
  43.6 9.7 %shard_map.88 = f32[36,128]{1,0:T(8,128)S(1)} custom-call(s32[18]{0:T(128)S(1)} %get-tuple-element.12.count_ref, s32[18,40]{1,0:T(8,128)S(1)} %fusion.5.list_ref, s32[36]{0:T(128)S(1)} %get-tuple-element.15.live_ref, bf16[18,256,256]{2,1,0:T(8,128)(2,1)S(1)} %get-tuple-element.6.main_ref, bf16[4736,256]{1,0:T(8,128)(2,1)S(1)} %copy-done.1, ...), custom_call_target="tpu_custom_call" | custom-call | tf_op jit(solution)/shard_map/pallas_call | solution.py:356
  53.3 0.7 all_to_all.15
  54.0 98.8 %all-to-all-start.1 = ((f32[16,1,288]{2,1,0:T(1,128)}), f32[16,1,288]{2,1,0:T(1,128)S(1)}, u32[]{:S(2)}, u32[]{:S(2)}) async-start(f32[16,1,288]{2,1,0:T(1,128)} %all_to_all.15), calls=%async_computation.1 | async-start | bytes 49152 | tf_op jit(solution)/shard_map/all_to_all | solution.py:370
  152.8 0.1 multiply_select_fusion
  152.9 0.7 collective-permute-start.5
  153.6 1.3 collective-permute-start.6
  154.8 3.5 %all-to-all-done.1 = f32[16,1,288]{2,1,0:T(1,128)S(1)} async-done(((f32[16,1,288]{2,1,0:T(1,128)}), f32[16,1,288]{2,1,0:T(1,128)S(1)}, u32[]{:S(2)}, u32[]{:S(2)}) %all-to-all-start.1) | async-done | bytes 18464 | tf_op jit(solution)/shard_map/all_to_all | solution.py:370
  158.5 0.0 copy-done.6
  158.5 0.6 add_select_fusion.2
  159.1 0.0 collective-permute-done.5
  159.1 20.8 %collective-permute-done.6 = f32[4608]{0:T(1024)S(1)} collective-permute-done((f32[4608]{0:T(1024)S(1)}, f32[4608]{0:T(1024)S(1)}, u32[]{:S(2)}, u32[]{:S(2)}) %collective-permute-start.6) | collective-permute-done | bytes 18464 | tf_op jit(solution)/shard_map/ppermute | solution.py:345
  179.8 0.6 select_select_fusion
  (12 shorter events, 0.1 us)
Async XLA Ops:
  5.7 7.6 %copy-start.5 = (s32[18,28]{1,0:T(8,128)S(1)}, s32[18,28]{1,0:T(8,128)}, u32[]{:S(2)}) copy-start(s32[18,28]{1,0:T(8,128)} %param.10) | copy-start | bytes 6052
  5.7 7.6 %copy-start.9 = (s32[18]{0:T(128)S(1)}, s32[18]{0:T(128)}, u32[]{:S(2)}) copy-start(s32[18]{0:T(128)} %param.11) | copy-start | bytes 220
  5.7 8.2 %copy-start.8 = (s32[18]{0:T(128)S(1)}, s32[18]{0:T(128)}, u32[]{:S(2)}) copy-start(s32[18]{0:T(128)} %param.13) | copy-start | bytes 220
  5.7 8.9 %copy-start.2 = (f32[4608,64]{0,1:T(8,128)S(1)}, f32[4608,64]{0,1:T(8,128)}, u32[]{:S(2)}) copy-start(f32[4608,64]{0,1:T(8,128)} %param.7) | copy-start | bytes 3538948
  5.7 25.3 %all-to-all-start = ((f32[16,152,128]{2,1,0:T(8,128)}), f32[16,152,128]{2,1,0:T(8,128)}, u32[]{:S(2)}, u32[]{:S(2)}) async-start(f32[16,152,128]{2,1,0:T(8,128)} %broadcast_in_dim.117), calls=%async_computation | async-start | bytes 2490368 | tf_op jit(solution)/shard_map/all_to_all | solution.py:266
  14.9 2.2 %copy-start.3 = (f32[18,256]{1,0:T(8,128)}, f32[18,256]{1,0:T(8,128)S(1)}, u32[]{:S(2)}) copy-start(f32[18,256]{1,0:T(8,128)S(1)} %get-tuple-element.9) | copy-start | bytes 55300
  31.0 10.7 %copy-start.7 = (s32[18]{0:T(128)S(1)}, s32[18]{0:T(128)}, u32[]{:S(2)}) copy-start(s32[18]{0:T(128)} %param.12) | copy-start | bytes 220
  31.0 10.9 %copy-start.4 = (f32[18,256]{1,0:T(8,128)S(1)}, f32[18,256]{1,0:T(8,128)}, u32[]{:S(2)}) copy-start(f32[18,256]{1,0:T(8,128)} %copy-done.3) | copy-start | bytes 55300
  36.9 1.4 copy-start
  38.3 3.4 %collective-permute-start = (f32[18,256]{1,0:T(8,128)S(1)}, f32[18,256]{1,0:T(8,128)S(1)}, u32[]{:S(2)}, u32[]{:S(2)}) collective-permute-start(f32[18,256]{1,0:T(8,128)S(1)} %get-tuple-element.7), channel_id=1, source_target_pairs={{14,15},{15,0},{0,1},{1,2},{2,8},{8,14},{31,16},{16,17},{17,18},{1... | collective-permute-start | bytes 55304 | tf_op jit(solution)/shard_map/ppermute | solution.py:326
  39.0 2.8 %collective-permute-start.1 = (f32[18,256]{1,0:T(8,128)S(1)}, f32[18,256]{1,0:T(8,128)S(1)}, u32[]{:S(2)}, u32[]{:S(2)}) collective-permute-start(f32[18,256]{1,0:T(8,128)S(1)} %get-tuple-element.7), channel_id=1, source_target_pairs={{14,0},{15,1},{0,2},{1,8},{2,14},{8,15},{31,17},{16,18},{17,19},{1... | collective-permute-start | bytes 55304 | tf_op jit(solution)/shard_map/ppermute | solution.py:326
  39.7 2.1 %collective-permute-start.2 = (f32[18,256]{1,0:T(8,128)S(1)}, f32[18,256]{1,0:T(8,128)S(1)}, u32[]{:S(2)}, u32[]{:S(2)}) collective-permute-start(f32[18,256]{1,0:T(8,128)S(1)} %get-tuple-element.7), channel_id=1, source_target_pairs={{14,1},{15,2},{0,8},{1,14},{2,15},{8,0},{31,18},{16,19},{17,25},{1... | collective-permute-start | bytes 55304 | tf_op jit(solution)/shard_map/ppermute | solution.py:326
  40.3 1.5 collective-permute-start.3
  41.0 0.8 collective-permute-start.4
  41.9 1.7 copy-start.1
  43.6 114.9 %copy-start.6 = (f32[288]{0:T(512)S(1)}, f32[288]{0:T(512)}, u32[]{:S(2)}) copy-start(f32[288]{0:T(512)} %param.9) | copy-start | bytes 3460
  54.0 104.4 %all-to-all-start.1 = ((f32[16,1,288]{2,1,0:T(1,128)}), f32[16,1,288]{2,1,0:T(1,128)S(1)}, u32[]{:S(2)}, u32[]{:S(2)}) async-start(f32[16,1,288]{2,1,0:T(1,128)} %all_to_all.15), calls=%async_computation.1 | async-start | bytes 49152 | tf_op jit(solution)/shard_map/all_to_all | solution.py:370
  152.9 6.2 %collective-permute-start.5 = (f32[4608]{0:T(1024)S(1)}, f32[4608]{0:T(1024)S(1)}, u32[]{:S(2)}, u32[]{:S(2)}) collective-permute-start(f32[4608]{0:T(1024)S(1)} %reshape.112), channel_id=1, source_target_pairs={{14,10},{15,11},{0,12},{1,13},{31,27},{16,28},{17,29},{18,30},{32,... | collective-permute-start | bytes 55304 | tf_op jit(solution)/shard_map/ppermute | solution.py:345
  153.6 26.3 %collective-permute-start.6 = (f32[4608]{0:T(1024)S(1)}, f32[4608]{0:T(1024)S(1)}, u32[]{:S(2)}, u32[]{:S(2)}) collective-permute-start(f32[4608]{0:T(1024)S(1)} %reshape.112), channel_id=1, source_target_pairs={{14,3},{15,4},{0,5},{1,6},{2,7},{8,9},{31,20},{16,21},{17,22},{18,... | collective-permute-start | bytes 55304 | tf_op jit(solution)/shard_map/ppermute | solution.py:345

commit v2 on v1

v2 whole, which is shorter than its diff:
```python
import functools
import math

import jax
import jax.numpy as jnp
from jax import lax
from jax.experimental import pallas as pl
from jax.experimental.pallas import tpu as pltpu
from jax.sharding import PartitionSpec as P

entropy = 0.1
scale = math.log2(math.e) / entropy
ln2 = math.log(2.0)
nothing = -1e30
floor = -1e25
unit_rows = 64
group = 12
f32 = jnp.float32
bf16 = jnp.bfloat16


def pieces(a):
    first = a.astype(bf16).astype(f32)
    rest = a - first
    second = rest.astype(bf16).astype(f32)
    return first, second, rest - second

def extra_rows(bias):
    place = lax.broadcasted_iota(jnp.int32, (64, bias.shape[1]), 0)
    block = jnp.where(place < 3, 1.0, 0.0)
    for k, piece in enumerate(pieces(bias)):
        block = jnp.where(place == 3 + k, piece, block)
    return block.astype(bf16)

def prepare_sources(points_ref, main_ref, bias_ref):
    tiles, depth, tile = main_ref.shape
    for s in range(tiles):
        x = points_ref[:, s * tile : (s + 1) * tile]
        high = x.astype(bf16)
        low = (x - high.astype(f32)).astype(bf16)
        bias = (-0.5 * scale) * jnp.sum(x * x, axis=0, keepdims=True)
        main_ref[s, 0:64, :] = high
        main_ref[s, 64:128, :] = high
        main_ref[s, 128:192, :] = low
        main_ref[s, 192:256, :] = extra_rows(bias)
        bias_ref[s : s + 1, :] = bias

def unpack_targets(wire_ref, operand_ref):
    lane = lax.broadcasted_iota(jnp.int32, (144, 128), 1)
    front = lane < 64
    sublane = lax.broadcasted_iota(jnp.int32, (16, 256), 0)
    r16 = lax.broadcasted_iota(jnp.int32, (16, 128), 0)
    l16 = lax.broadcasted_iota(jnp.int32, (16, 128), 1)
    pick = jnp.where((l16 == r16 + 64) & (r16 < 6), 1.0, 0.0).astype(bf16)

    def columns(row):
        stacked = jnp.where(sublane < 6, 1.0, 0.0)
        for k, piece in enumerate(pieces(row)):
            stacked = jnp.where(sublane == k, piece, stacked)
        return lax.dot_general(
            stacked.astype(bf16), pick, (((0,), (0,)), ((), ())), preferred_element_type=f32
        )[0:144]

    for m in range(wire_ref.shape[0]):
        both = wire_ref[m, 0:144, :]
        high = both.astype(bf16).astype(f32)
        low = both - high
        high_back = pltpu.roll(high, 64, 1)
        low_back = pltpu.roll(low, 64, 1)
        tail = wire_ref[m, 144:152, :]
        extra_a = columns(jnp.concatenate([tail[0:1], tail[1:2]], axis=1))
        extra_b = columns(jnp.concatenate([tail[2:3], tail[3:4]], axis=1))
        a = m * 288
        b = a + 144
        operand_ref[a : a + 144, 0:128] = jnp.where(front, high, low_back).astype(bf16)
        operand_ref[a : a + 144, 128:256] = jnp.where(front, high, extra_a).astype(bf16)
        operand_ref[b : b + 144, 0:128] = jnp.where(front, high_back, low).astype(bf16)
        operand_ref[b : b + 144, 128:256] = jnp.where(front, high_back, extra_b).astype(bf16)
    rows = wire_ref.shape[0] * 288
    dummy_lane = lax.broadcasted_iota(jnp.int32, (unit_rows, 256), 1)
    operand_ref[rows : rows + unit_rows, :] = jnp.where(dummy_lane == 192, nothing, 0.0).astype(bf16)

def pipeline(item_ref, list_ref, items, operand_ref, weights_ref, buffers, visit):
    per = list_ref.shape[1] // group

    def where(i):
        code = item_ref[i]
        s = code // per
        return s, (code - s * per) * group

    def units(i):
        s, first = where(i)
        return [list_ref[s, first + k] for k in range(group)]

    def multiply(i, buffer):
        s, first = where(i)
        rows = jnp.concatenate(
            [
                operand_ref[pl.ds(pl.multiple_of(u * unit_rows, unit_rows), unit_rows), :]
                for u in units(i)
            ],
            axis=0,
        )
        held = jnp.minimum(s, weights_ref.shape[0] - 1)
        buffer[...] = jnp.dot(rows, weights_ref[held], preferred_element_type=f32)

    one, two = buffers
    multiply(0, one)

    def step(j, carry):
        multiply(2 * j + 1, two)
        visit(jnp.minimum(where(2 * j)[0], weights_ref.shape[0] - 1), units(2 * j), one)
        multiply(2 * j + 2, one)
        visit(jnp.minimum(where(2 * j + 1)[0], weights_ref.shape[0] - 1), units(2 * j + 1), two)
        return carry

    lax.fori_loop(0, (items + 1) // 2, step, 0)

def row_pass(items_ref, item_ref, count_ref, list_ref, wire_ref, main_ref, need_ref, lse_ref, operand_ref, one, two, total_ref):
    tiles, depth, tile = main_ref.shape
    unpack_targets(wire_ref, operand_ref)
    total_ref[...] = jnp.zeros_like(total_ref)

    def visit(s, units, buffer):
        part = jnp.exp2(buffer[...]).reshape(4, unit_rows * group // 32, 8, tile)
        total_ref[s] += jnp.sum(jnp.sum(part, axis=1), axis=0)

    pipeline(item_ref, list_ref, items_ref[0], operand_ref, main_ref, (one, two), visit)
    total = jnp.sum(total_ref[...], axis=1)
    lse_ref[...] = jnp.where(total > 0.0, jnp.log2(jnp.maximum(total, 1e-37)), nothing)
    fine = (total > 1e-25) & (total < 1e30)
    bad = jnp.where(fine, 0.0, need_ref[...])

    @pl.when(jnp.max(bad) > 0.0)
    def _():
        def one_tile(s, carry):
            weights = main_ref[s]

            def step(i, state):
                high, total = state
                unit = list_ref[s, i]
                rows = operand_ref[pl.ds(pl.multiple_of(unit * unit_rows, unit_rows), unit_rows), :]
                score = jnp.dot(rows, weights, preferred_element_type=f32)
                score = score.reshape(unit_rows // 8, 8, tile)
                new = jnp.maximum(high, jnp.max(score, axis=0))
                total = total * jnp.exp2(high - new) + jnp.sum(jnp.exp2(score - new[None]), axis=0)
                return new, total

            start = (jnp.full((8, tile), floor, f32), jnp.zeros((8, tile), f32))
            high, total = lax.fori_loop(0, count_ref[s], step, start)
            top = jnp.max(high, axis=0, keepdims=True)
            total = jnp.sum(total * jnp.exp2(high - top), axis=0, keepdims=True)
            lse_ref[pl.ds(s, 1), :] = jnp.where(
                total > 0.0, top + jnp.log2(jnp.maximum(total, 1e-37)), nothing
            )
            return carry

        lax.fori_loop(0, tiles, one_tile, 0)

def column_pass(items_ref, item_ref, count_ref, list_ref, main_ref, operand_ref, bias_ref, need_ref, out_ref, one, two, weights_ref, total_ref, high_ref):
    tiles, depth, tile = main_ref.shape
    rows = total_ref.shape[0]
    weights_ref[:, 0:192, :] = main_ref[:, 0:192, :]
    for s in range(tiles):
        weights_ref[s, 192:256, :] = extra_rows(bias_ref[s : s + 1, :])
    total_ref[...] = jnp.zeros_like(total_ref)

    def visit(s, units, buffer):
        for k, u in enumerate(units):
            where = pl.ds(pl.multiple_of(u * unit_rows, unit_rows), unit_rows)
            part = jnp.exp2(buffer[k * unit_rows : (k + 1) * unit_rows, :])
            total_ref[where, :] += part[:, 0:128] + part[:, 128:256]

    pipeline(item_ref, list_ref, items_ref[0], operand_ref, weights_ref, (one, two), visit)
    eye = lax.broadcasted_iota(jnp.int32, (128, 128), 0) == lax.broadcasted_iota(jnp.int32, (128, 128), 1)

    def to_row(column):
        return jnp.sum(jnp.where(eye, column, 0.0), axis=0, keepdims=True)

    bad = jnp.zeros((1, 128), f32)
    for u in range(out_ref.shape[0]):
        sums = to_row(jnp.sum(total_ref[u * 128 : (u + 1) * 128, :], axis=1, keepdims=True))
        out_ref[u : u + 1, :] = jnp.where(sums > 0.0, jnp.log2(jnp.maximum(sums, 1e-37)), nothing)
        bad = jnp.maximum(bad, jnp.where(sums > 1e-25, 0.0, need_ref[u : u + 1, :]))

    @pl.when(jnp.max(bad) > 0.0)
    def _():
        total_ref[...] = jnp.zeros_like(total_ref)
        high_ref[...] = jnp.full_like(high_ref, floor)

        def one_tile(s, carry):
            def step(i, inner):
                unit = list_ref[s, i]
                where = pl.ds(pl.multiple_of(unit * unit_rows, unit_rows), unit_rows)
                score = jnp.dot(operand_ref[where, :], weights_ref[s], preferred_element_type=f32)
                a, b = score[:, 0:128], score[:, 128:256]
                old = high_ref[where, :]
                new = jnp.maximum(old, jnp.maximum(a, b))
                high_ref[where, :] = new
                total_ref[where, :] = (
                    total_ref[where, :] * jnp.exp2(old - new) + jnp.exp2(a - new) + jnp.exp2(b - new)
                )
                return inner

            lax.fori_loop(0, count_ref[s], step, 0)
            return carry

        lax.fori_loop(0, tiles, one_tile, 0)

        def finish(u, carry):
            where = pl.ds(pl.multiple_of(u * 128, 128), 128)
            high = high_ref[where, :]
            top = jnp.max(high, axis=1, keepdims=True)
            sums = to_row(jnp.sum(total_ref[where, :] * jnp.exp2(high - top), axis=1, keepdims=True))
            out_ref[pl.ds(u, 1), :] = jnp.where(
                sums > 0.0, to_row(top) + jnp.log2(jnp.maximum(sums, 1e-37)), nothing
            )
            return carry

        lax.fori_loop(0, out_ref.shape[0], finish, 0)


def log_sum(parts):
    top = functools.reduce(jnp.maximum, parts)
    total = sum(jnp.exp2(p - top) for p in parts)
    return top + jnp.log2(total)


def work_lists(partners, partner_count, dst_count, col_here):
    src_tiles, slots = partners.shape
    dst_tiles = dst_count.shape[0]
    per_tile = 256 // unit_rows
    units = dst_tiles * per_tile
    per = -(-units // group)
    slot_on = jnp.arange(slots, dtype=jnp.int32)[None, :] < partner_count[:, None]
    local = jnp.where(slot_on, partners - col_here * dst_tiles, -1)
    unit_ids = jnp.arange(units, dtype=jnp.int32)
    unit_tile = unit_ids // per_tile
    live = jnp.repeat(dst_count, per_tile) > (unit_ids % per_tile) * unit_rows
    active = jnp.any(local[:, :, None] == unit_tile[None, None, :], axis=1) & live[None, :]
    earlier = unit_ids[:, None] < unit_ids[None, :]
    rank = jnp.sum((active[:, :, None] & earlier[None]).astype(jnp.int32), axis=1)
    counts = jnp.sum(active.astype(jnp.int32), axis=1)
    order = jnp.arange(per * group, dtype=jnp.int32)
    listed = jnp.sum(
        jnp.where(
            active[:, :, None] & (rank[:, :, None] == order[None, None, :]),
            unit_ids[None, :, None] - units,
            0,
        ),
        axis=1,
    ) + units
    listed = jnp.concatenate([listed, jnp.full((1, per * group), units, jnp.int32)], axis=0)
    chunks = (counts + group - 1) // group
    tile_ids = jnp.arange(src_tiles, dtype=jnp.int32)
    first = jnp.sum(jnp.where(tile_ids[None, :] < tile_ids[:, None], chunks[None, :], 0), axis=1)
    within = jnp.arange(per, dtype=jnp.int32)
    spot = jnp.where(within[None, :] < chunks[:, None], first[:, None] + within[None, :], -1)
    code = tile_ids[:, None] * per + within[None, :] - src_tiles * per
    length = src_tiles * per + 2
    hit = spot.reshape(-1)[:, None] == jnp.arange(length, dtype=jnp.int32)[None, :]
    items = jnp.sum(jnp.where(hit, code.reshape(-1)[:, None], 0), axis=0) + src_tiles * per
    wanted = jnp.any(local[:, :, None] == jnp.arange(dst_tiles, dtype=jnp.int32), axis=1)
    return jnp.sum(chunks)[None], items, counts, listed, wanted


def shards(src_points, dst_points, dst_potential, partners, partner_count, src_count, dst_count):
    src_tiles = src_count.shape[0]
    dst_tiles = dst_count.shape[0]
    tile = src_points.shape[0] // src_tiles
    slots = partners.shape[1]
    rows = lax.axis_size("row")
    cols = lax.axis_size("col")
    row_here = lax.axis_index("row")
    col_here = lax.axis_index("col")
    share = dst_points.shape[0]
    points = dst_tiles * tile
    smem = pl.BlockSpec(memory_space=pltpu.SMEM)
    vmem = pl.BlockSpec(memory_space=pltpu.VMEM)
    params = pltpu.CompilerParams(vmem_limit_bytes=20 * 1024 * 1024)
    buffers = [pltpu.VMEM((unit_rows * group, tile), f32)] * 2

    spot = row_here * share + jnp.arange(share, dtype=jnp.int32)
    spot_tile = spot // tile
    spot_count = jnp.sum(
        jnp.where(
            spot_tile[:, None] == jnp.arange(dst_tiles, dtype=jnp.int32)[None, :],
            dst_count[None, :],
            0,
        ),
        axis=1,
    )
    mine_valid = spot - spot_tile * tile < spot_count
    level = scale * (dst_potential - 0.5 * jnp.sum(dst_points * dst_points, axis=1))
    level = jnp.where(mine_valid, level, nothing)
    mid = share // 2
    packed = scale * jnp.concatenate([dst_points[:mid], dst_points[mid:]], axis=1)
    tail = jnp.pad(level.reshape(2, mid), ((0, 0), (0, 256 - mid))).reshape(4, 128)
    wire = jnp.concatenate([packed, tail, jnp.zeros((4, 128), f32)], axis=0)
    gathered = lax.all_to_all(
        jnp.broadcast_to(wire[None], (rows,) + wire.shape), "row", 0, 0
    )

    main, bias = pl.pallas_call(
        prepare_sources,
        out_shape=(
            jax.ShapeDtypeStruct((src_tiles, 256, tile), bf16),
            jax.ShapeDtypeStruct((src_tiles, tile), f32),
        ),
        in_specs=[vmem],
        out_specs=(vmem, vmem),
        compiler_params=params,
    )(src_points.T)

    total_items, items, counts, listed, wanted = work_lists(
        partners, partner_count, dst_count, col_here
    )
    place = jnp.arange(tile, dtype=jnp.int32)
    src_live = place[None, :] < src_count[:, None]
    dst_live = place[None, :] < dst_count[:, None]
    src_need = jnp.where(src_live & (counts > 0)[:, None], 1.0, 0.0)
    dst_need = jnp.where(dst_live & jnp.any(wanted, axis=0)[:, None], 1.0, 0.0)
    dst_need = dst_need.reshape(points // 128, 128)

    lse, operand = pl.pallas_call(
        row_pass,
        out_shape=(
            jax.ShapeDtypeStruct((src_tiles, tile), f32),
            jax.ShapeDtypeStruct((points + unit_rows, 256), bf16),
        ),
        in_specs=[smem] * 4 + [vmem] * 3,
        out_specs=(vmem, vmem),
        scratch_shapes=buffers + [pltpu.VMEM((src_tiles, 8, tile), f32)],
        compiler_params=params,
    )(total_items, items, counts, listed, gathered, main, src_need)

    reach = -(-slots // dst_tiles)
    steps = [d % cols for d in range(-reach, reach + 1)] + [cols // 2]
    idle = [d for d in range(cols) if d not in steps]
    mates = len(steps)

    def to(row, src, dst):
        return (row * cols + (row + src) % cols, row * cols + (row + dst) % cols)

    parts = [lse]
    for turn in range(1, mates):
        hops = [
            to(r, steps[a], steps[(a + turn) % mates]) for r in range(rows) for a in range(mates)
        ]
        parts.append(lax.ppermute(lse, ("row", "col"), hops))
    row_lse = log_sum(parts)
    counted = src_count.astype(f32)
    all_src = src_tiles * rows
    potential = jnp.where(
        src_live,
        entropy * (-jnp.log(counted)[:, None] - math.log(all_src) - ln2 * row_lse),
        0.0,
    )
    shared = potential.reshape(-1)
    member = functools.reduce(
        jnp.logical_or, [(col_here - row_here) % cols == d for d in steps]
    )
    src_potential = jnp.where(member, shared, 0.0)
    for begin in range(0, len(idle), mates):
        chunk = idle[begin : begin + mates]
        hops = [to(r, steps[a], d) for r in range(rows) for a, d in enumerate(chunk)]
        got = lax.ppermute(shared, ("row", "col"), hops)
        here = functools.reduce(
            jnp.logical_or, [(col_here - row_here) % cols == d for d in chunk]
        )
        src_potential = jnp.where(here, got, src_potential)

    mass_bias = jnp.where(
        src_live,
        bias - row_lse - jnp.log2(counted)[:, None] - math.log2(all_src),
        nothing,
    )
    col_part = pl.pallas_call(
        column_pass,
        out_shape=jax.ShapeDtypeStruct((points // 128, 128), f32),
        in_specs=[smem] * 4 + [vmem] * 4,
        out_specs=vmem,
        scratch_shapes=buffers
        + [
            pltpu.VMEM((src_tiles, 256, tile), bf16),
            pltpu.VMEM((points + unit_rows, 128), f32),
            pltpu.VMEM((points + unit_rows, 128), f32),
        ],
        compiler_params=params,
    )(total_items, items, counts, listed, main, operand, mass_bias, dst_need)

    shared_out = lax.all_to_all(col_part.reshape(rows, share), "row", 0, 0)
    top = jnp.max(shared_out, axis=0)
    col_log = top + jnp.log2(jnp.sum(jnp.exp2(shared_out - top[None]), axis=0))
    dst_new = jnp.where(
        mine_valid & (top > 0.5 * nothing),
        entropy
        * (-jnp.log(spot_count.astype(f32)) - math.log(dst_tiles * cols) - ln2 * col_log)
        + dst_potential,
        0.0,
    )
    return src_potential, dst_new


def solution(mesh):
    in_specs = (
        P("row", None),
        P(("col", "row"), None),
        P(("col", "row")),
        P("row", None),
        P("row"),
        P("row"),
        P("col"),
    )
    out_specs = (P("row"), P(("col", "row")))
    return jax.shard_map(shards, mesh=mesh, in_specs=in_specs, out_specs=out_specs, check_vma=False)
```

time: 181 us -> 236 us (1.30)
  starting transfers between devices: 112 us -> 193 us
  waiting for transfers between devices: 38.1 us -> 13.2 us
  Pallas kernels: 16 us -> 6.68 us
  other arithmetic: 6.75 us -> 11.4 us
  local copies, waits for them, and re-layouts: 7.06 us -> 10.6 us
    all_to_all x1, starting transfers between devices: 98.8 us -> 180 us  [shards(): shared_out = lax.all_to_all(col_part.reshape(rows, share), 'row', 0, 0)]
    ppermute x2, waiting for transfers between devices: 20.8 us -> 4.17 us  [shards(): got = lax.ppermute(shared, ('row', 'col'), hops)]
    all_to_all x1, waiting for transfers between devices: 13.8 us -> 5.47 us  [shards(): lax.all_to_all(jnp.broadcast_to(wire[None], (rows,) + wire.shape), 'row',...]
    pallas_call x1, Pallas kernels: 9.69 us -> 2.86 us  [shards(): pl.pallas_call(column_pass, out_shape=jax.ShapeDtypeStruct((points // 128...]
    reduce_sum x3 -> x6, other arithmetic: 0.68 us -> 4.44 us  [the longest x1 1.3 us: work_lists(): jnp.sum(jnp.where(active[:, :, None] & (rank[:, :, None] == order[None, N...]
    pallas_call x1, Pallas kernels: 5.93 us -> 3.49 us  [shards(): pl.pallas_call(row_pass, out_shape=(jax.ShapeDtypeStruct((src_tiles, tile...]
  transfers between devices with their start and end apart: 9 -> 9, of which waited for: 3 -> 3; matrix products, arithmetic and copies ran while one was open for 2% -> 5% of each run, Pallas kernels for 0% -> 0%
where the time goes in v2:
time: 236 us
  starting transfers between devices  193 us (82%)
  waiting for transfers between devices  13.2 us (6%)
  other arithmetic  11.4 us (5%)
  local copies, waits for them, and re-layouts  10.6 us (4%)
  Pallas kernels  6.68 us (3%)
    all_to_all x1, starting transfers between devices, shards(): shared_out = lax.all_to_all(col_part.reshape(rows, share), 'row', 0, 0)  180 us
    all_to_all x1, starting transfers between devices, shards(): lax.all_to_all(jnp.broadcast_to(wire[None], (rows,) + wire.shape), 'row',...  7.57 us
    all_to_all x1, waiting for transfers between devices, shards(): lax.all_to_all(jnp.broadcast_to(wire[None], (rows,) + wire.shape), 'row',...  5.47 us
  transfers between devices with their start and end apart: 9, of which 3 were waited for; matrix products, arithmetic and copies ran while one was open for 5% of the time, Pallas kernels for 0%

profile of v2, /device:TPU:6, one launch (start us, length us, event | category | flops | bytes accessed | tf_op | source)
XLA Modules:
  0.0 235.6 jit_solution(1429956401736058867)
XLA Ops:
  0.6 0.9 multiply_reduce_fusion
  1.6 1.0 fusion.14
  2.6 0.7 select_reduce_fusion.2
  3.3 0.0 copy-start.5
  3.3 0.7 multiply_select_fusion.1
  4.0 0.1 reshape.197
  4.1 0.1 copy.15
  4.3 0.1 pad.8.clone
  4.4 0.1 maximum_maximum_fusion
  4.4 0.1 copy.16
  4.5 1.1 broadcast_in_dim.153
  5.7 7.6 %all-to-all-start = ((f32[16,152,128]{2,1,0:T(8,128)}), f32[16,152,128]{2,1,0:T(8,128)}, u32[]{:S(2)}, u32[]{:S(2)}) async-start(f32[16,152,128]{2,1,0:T(8,128)} %broadcast_in_dim.153), calls=%async_computation | async-start | bytes 2490368 | tf_op jit(solution)/shard_map/all_to_all | solution.py:300
  13.3 0.5 iota_add_fusion.1
  13.9 0.5 multiply_add_fusion.1
  14.4 0.1 subtract_select_fusion
  14.5 0.7 fusion.1
  15.2 0.2 compare_reduce_fusion
  15.4 0.1 broadcast_in_dim.140
  15.5 0.1 reshape.196
  15.6 0.7 convert_reduce_fusion.1
  16.3 0.7 fusion.13
  16.9 0.1 select_reduce_fusion.3
  17.1 0.1 add_select_fusion.1
  17.1 0.6 select_n.161
  17.7 0.1 add_add_fusion
  17.8 0.6 sub.130
  18.4 0.3 shard_map.86
  18.8 0.6 copy-done.3
  19.4 0.7 and.140
  20.1 0.1 and.141
  20.2 0.6 lt.172
  20.9 0.7 lt.174
  21.6 0.1 lt.175
  21.7 0.9 convert_reduce_fusion
  22.6 1.3 select_reduce_fusion
  23.9 0.7 select_reduce_fusion.1
  24.7 0.7 fusion.6.need_ref
  25.4 0.1 and_select_fusion.need_ref
  25.5 5.5 %all-to-all-done.wire_ref = f32[16,152,128]{2,1,0:T(8,128)} async-done(((f32[16,152,128]{2,1,0:T(8,128)}), f32[16,152,128]{2,1,0:T(8,128)}, u32[]{:S(2)}, u32[]{:S(2)}) %all-to-all-start) | async-done | bytes 1245216 | tf_op jit(solution)/shard_map/all_to_all | solution.py:300
  31.0 3.5 %shard_map.87 = (f32[18,256]{1,0:T(8,128)S(1)}, bf16[4672,256]{1,0:T(8,128)(2,1)S(1)}) custom-call(s32[1]{0:T(128)} %bitcast.items_ref, s32[110]{0:T(128)S(1)} %broadcast_add_fusion.1.item_ref, s32[18]{0:T(128)S(1)} %get-tuple-element.14.count_ref, s32[19,72]{1,0:T(8,128)S(1)} %concatenate.9.list_ref, f32[16,152,128]{2,1,0:T(8,128)} %all-to-all-done.wire_ref, ...), custom_call_target="tpu_custom_call" | custom-call | tf_op jit(solution)/shard_map/pallas_call | solution.py:325
  34.5 1.4 copy-done
  35.9 0.7 collective-permute-start
  36.6 0.7 collective-permute-start.1
  37.2 0.7 collective-permute-start.2
  37.9 0.7 collective-permute-start.3
  38.6 0.7 collective-permute-start.4
  39.3 0.0 collective-permute-done
  39.4 0.0 collective-permute-done.1
  39.4 0.0 collective-permute-done.2
  39.4 0.0 collective-permute-done.3
  39.4 0.0 collective-permute-done.4
  39.4 0.1 add_select_fusion
  39.5 1.7 copy-done.1
  41.2 2.9 %shard_map.88 = f32[36,128]{1,0:T(8,128)S(1)} custom-call(s32[1]{0:T(128)} %bitcast.items_ref, s32[110]{0:T(128)S(1)} %broadcast_add_fusion.1.item_ref, s32[18]{0:T(128)S(1)} %get-tuple-element.14.count_ref, s32[19,72]{1,0:T(8,128)S(1)} %concatenate.9.list_ref, bf16[18,256,256]{2,1,0:T(8,128)(2,1)S(1)} %get-tuple-element.6.main_ref, ...), custom_call_target="tpu_custom_call" | custom-call | tf_op jit(solution)/shard_map/pallas_call | solution.py:378
  44.0 0.7 all_to_all.15
  44.7 179.8 %all-to-all-start.1 = ((f32[16,1,288]{2,1,0:T(1,128)}), f32[16,1,288]{2,1,0:T(1,128)S(1)}, u32[]{:S(2)}, u32[]{:S(2)}) async-start(f32[16,1,288]{2,1,0:T(1,128)} %all_to_all.15), calls=%async_computation.1 | async-start | bytes 49152 | tf_op jit(solution)/shard_map/all_to_all | solution.py:392
  224.5 0.1 multiply_select_fusion
  224.6 0.7 collective-permute-start.5
  225.2 1.3 collective-permute-start.6
  226.5 3.6 %all-to-all-done.1 = f32[16,1,288]{2,1,0:T(1,128)S(1)} async-done(((f32[16,1,288]{2,1,0:T(1,128)}), f32[16,1,288]{2,1,0:T(1,128)S(1)}, u32[]{:S(2)}, u32[]{:S(2)}) %all-to-all-start.1) | async-done | bytes 18464 | tf_op jit(solution)/shard_map/all_to_all | solution.py:392
  230.2 0.6 add_select_fusion.3
  230.8 0.0 collective-permute-done.5
  230.8 4.2 %collective-permute-done.6 = f32[4608]{0:T(1024)S(1)} collective-permute-done((f32[4608]{0:T(1024)S(1)}, f32[4608]{0:T(1024)S(1)}, u32[]{:S(2)}, u32[]{:S(2)}) %collective-permute-start.6) | collective-permute-done | bytes 18464 | tf_op jit(solution)/shard_map/ppermute | solution.py:367
  235.0 0.6 select_select_fusion
  (38 shorter events, 0.2 us)
Async XLA Ops:
  3.3 2.4 %copy-start.5 = (s32[288]{0:T(512)}, s32[288]{0:T(512)S(1)}, u32[]{:S(2)}) copy-start(s32[288]{0:T(512)S(1)} %select_reduce_fusion.2) | copy-start | bytes 3460
  5.7 8.7 %copy-start.7 = (s32[18,28]{1,0:T(8,128)S(1)}, s32[18,28]{1,0:T(8,128)}, u32[]{:S(2)}) copy-start(s32[18,28]{1,0:T(8,128)} %param.10) | copy-start | bytes 6052
  5.7 8.7 %copy-start.11 = (s32[18]{0:T(128)S(1)}, s32[18]{0:T(128)}, u32[]{:S(2)}) copy-start(s32[18]{0:T(128)} %param.11) | copy-start | bytes 220
  5.7 9.7 %copy-start.10 = (s32[18]{0:T(128)S(1)}, s32[18]{0:T(128)}, u32[]{:S(2)}) copy-start(s32[18]{0:T(128)} %param.13) | copy-start | bytes 220
  5.7 12.7 %copy-start.2 = (f32[4608,64]{0,1:T(8,128)S(1)}, f32[4608,64]{0,1:T(8,128)}, u32[]{:S(2)}) copy-start(f32[4608,64]{0,1:T(8,128)} %param.7) | copy-start | bytes 3538948
  5.7 25.3 %all-to-all-start = ((f32[16,152,128]{2,1,0:T(8,128)}), f32[16,152,128]{2,1,0:T(8,128)}, u32[]{:S(2)}, u32[]{:S(2)}) async-start(f32[16,152,128]{2,1,0:T(8,128)} %broadcast_in_dim.153), calls=%async_computation | async-start | bytes 2490368 | tf_op jit(solution)/shard_map/all_to_all | solution.py:300
  18.8 0.6 copy-start.3
  31.0 8.3 %copy-start.9 = (s32[18]{0:T(128)S(1)}, s32[18]{0:T(128)}, u32[]{:S(2)}) copy-start(s32[18]{0:T(128)} %param.12) | copy-start | bytes 220
  31.0 8.4 %copy-start.4 = (f32[18,256]{1,0:T(8,128)S(1)}, f32[18,256]{1,0:T(8,128)}, u32[]{:S(2)}) copy-start(f32[18,256]{1,0:T(8,128)} %copy-done.3) | copy-start | bytes 55300
  34.5 1.4 copy-start
  35.9 3.4 %collective-permute-start = (f32[18,256]{1,0:T(8,128)S(1)}, f32[18,256]{1,0:T(8,128)S(1)}, u32[]{:S(2)}, u32[]{:S(2)}) collective-permute-start(f32[18,256]{1,0:T(8,128)S(1)} %get-tuple-element.7), channel_id=1, source_target_pairs={{14,15},{15,0},{0,1},{1,2},{2,8},{8,14},{31,16},{16,17},{17,18},{1... | collective-permute-start | bytes 55304 | tf_op jit(solution)/shard_map/ppermute | solution.py:350
  36.6 2.8 %collective-permute-start.1 = (f32[18,256]{1,0:T(8,128)S(1)}, f32[18,256]{1,0:T(8,128)S(1)}, u32[]{:S(2)}, u32[]{:S(2)}) collective-permute-start(f32[18,256]{1,0:T(8,128)S(1)} %get-tuple-element.7), channel_id=1, source_target_pairs={{14,0},{15,1},{0,2},{1,8},{2,14},{8,15},{31,17},{16,18},{17,19},{1... | collective-permute-start | bytes 55304 | tf_op jit(solution)/shard_map/ppermute | solution.py:350
  37.2 2.1 collective-permute-start.2
  37.9 1.5 collective-permute-start.3
  38.6 0.8 collective-permute-start.4
  39.5 1.7 copy-start.1
  41.2 189.0 %copy-start.6 = (s32[288]{0:T(512)S(1)}, s32[288]{0:T(512)}, u32[]{:S(2)}) copy-start(s32[288]{0:T(512)} %copy-done.5) | copy-start | bytes 3460
  41.2 189.0 %copy-start.8 = (f32[288]{0:T(512)S(1)}, f32[288]{0:T(512)}, u32[]{:S(2)}) copy-start(f32[288]{0:T(512)} %param.9) | copy-start | bytes 3460
  44.7 185.4 %all-to-all-start.1 = ((f32[16,1,288]{2,1,0:T(1,128)}), f32[16,1,288]{2,1,0:T(1,128)S(1)}, u32[]{:S(2)}, u32[]{:S(2)}) async-start(f32[16,1,288]{2,1,0:T(1,128)} %all_to_all.15), calls=%async_computation.1 | async-start | bytes 49152 | tf_op jit(solution)/shard_map/all_to_all | solution.py:392
  224.6 6.2 %collective-permute-start.5 = (f32[4608]{0:T(1024)S(1)}, f32[4608]{0:T(1024)S(1)}, u32[]{:S(2)}, u32[]{:S(2)}) collective-permute-start(f32[4608]{0:T(1024)S(1)} %reshape.199), channel_id=1, source_target_pairs={{14,10},{15,11},{0,12},{1,13},{31,27},{16,28},{17,29},{18,30},{32,... | collective-permute-start | bytes 55304 | tf_op jit(solution)/shard_map/ppermute | solution.py:367
  225.2 9.7 %collective-permute-start.6 = (f32[4608]{0:T(1024)S(1)}, f32[4608]{0:T(1024)S(1)}, u32[]{:S(2)}, u32[]{:S(2)}) collective-permute-start(f32[4608]{0:T(1024)S(1)} %reshape.199), channel_id=1, source_target_pairs={{14,3},{15,4},{0,5},{1,6},{2,7},{8,9},{31,20},{16,21},{17,22},{18,... | collective-permute-start | bytes 55304 | tf_op jit(solution)/shard_map/ppermute | solution.py:367
